TPU v7x, 256 devices: a whole 4x4x8 slice. The times are simulated.
256 devices in a mesh: dp: 32 (over x_hi, z, core), blk: 8 (over x_lo, y).
Axes of the slice: x: 4 (x_hi: 2, x_lo: 2; x = x_hi * 2 + x_lo), y: 4, z: 8, core: 2. Of those that a mesh axis runs over, the one named last changes fastest.
Arguments:
- attn_cols: bfloat16 [32768, 7168], P('blk', 'dp'), may hold values from -6 to 6
- residual: bfloat16 [32768, 7168], P(('blk', 'dp')), may hold values from -80 to 80
- norm_gain: bfloat16 [7168], replicated, may hold values from 0.5 to 1.5
- router_weight: bfloat16 [7168, 32], replicated, may hold values from -0.0625 to 0.0625
- expert_ids: int32 [32768, 2], P(('blk', 'dp')), may hold values from 0 to 31, all different within a row; in each aligned block of 128 rows (0 to 127, 128 to 255, ...) at most 10 rows name the same one
- gate_weight: bfloat16 [32, 7168, 1024], P('dp', None, 'blk'), may hold values from -0.0625 to 0.0625
- up_weight: bfloat16 [32, 7168, 1024], P('dp', None, 'blk'), may hold values from -0.0625 to 0.0625
- down_weight: bfloat16 [32, 7168, 1024], P('dp', 'blk'), may hold values from -0.1875 to 0.1875
Outputs:
- layer_out: bfloat16 [32768, 7168], P(('blk', 'dp'))
Inputs may be any that keep to these rules, and one draw needn't show every extreme that they name: `expert_ids`: within each aligned block of 128 rows (the rows of one device) no expert is named by more than 10 rows, and in some block some expert is named by exactly 10 rows; the 2 experts of a row differ.
All inputs are finite; a program needn't handle non-finite values.
Results may differ from a plain program's by a relative error of at most 0.0044.
Values may be sent and summed in bfloat16 or wider, within the bound.
A program may use at most 192 MiB of HBM per device.

v0:
```python
import jax
import jax.numpy as jnp
from jax import lax
from jax.sharding import PartitionSpec as P


def body(
    attn_cols, residual, norm_gain, router_weight, expert_ids, gate_weight, up_weight, down_weight
):
    regrouped = lax.all_to_all(attn_cols, "dp", split_axis=0, concat_axis=1, tiled=True)
    tok_rows = residual.shape[0]
    width = residual.shape[1]
    fanout = expert_ids.shape[1]
    experts = router_weight.shape[1]
    exp_local = gate_weight.shape[0]
    groups = lax.axis_size("dp")
    capacity = max(2, (5 * tok_rows * fanout + 4 * experts - 1) // (4 * experts))
    stream = residual.astype(jnp.float32) + regrouped.astype(jnp.float32)
    meansq = jnp.mean(stream * stream, axis=1, keepdims=True)
    normed = (stream * lax.rsqrt(meansq + 1e-06) * norm_gain.astype(jnp.float32)).astype(
        jnp.bfloat16
    )
    affinity = jax.nn.sigmoid(jnp.dot(normed, router_weight, preferred_element_type=jnp.float32))
    chosen = jnp.take_along_axis(affinity, expert_ids, axis=1)
    weights = 2.5 * chosen / jnp.sum(chosen, axis=1, keepdims=True)
    flat_ids = expert_ids.reshape(-1)
    onehot = (flat_ids[:, None] == jnp.arange(experts, dtype=jnp.int32)[None, :]).astype(jnp.int32)
    before = jnp.cumsum(onehot, axis=0) - onehot
    ranks = jnp.sum(before * onehot, axis=1)
    slots = flat_ids * capacity + ranks
    outgoing = jnp.zeros((experts * capacity, width), jnp.bfloat16)
    outgoing = outgoing.at[slots].set(jnp.repeat(normed, fanout, axis=0))
    arrived = lax.all_to_all(
        outgoing.reshape(groups, exp_local * capacity, width),
        "dp",
        split_axis=0,
        concat_axis=0,
        tiled=True,
    )
    arrived = arrived.reshape(groups, exp_local, capacity, width)

    def project_in(piece):
        return jnp.einsum("secd,edf->secf", arrived, piece, preferred_element_type=jnp.float32)

    gated = project_in(lax.all_gather(gate_weight, "blk", axis=2, tiled=True))
    upward = project_in(lax.all_gather(up_weight, "blk", axis=2, tiled=True))
    hidden = (jax.nn.silu(gated) * upward).astype(jnp.bfloat16)
    produced = jnp.einsum(
        "secf,edf->secd",
        hidden,
        lax.all_gather(down_weight, "blk", axis=1, tiled=True),
        preferred_element_type=jnp.float32,
    ).astype(jnp.bfloat16)
    results = produced.reshape(groups, exp_local * capacity, width)
    returned = lax.all_to_all(results, "dp", split_axis=0, concat_axis=0, tiled=True).reshape(
        experts * capacity, width
    )
    picked = returned[slots].reshape(tok_rows, fanout, width)
    summed = stream
    for member in range(fanout):
        summed = summed + weights[:, member : member + 1] * picked[:, member].astype(jnp.float32)
    return summed.astype(jnp.bfloat16)


def solution(mesh):
    return jax.shard_map(
        body,
        mesh=mesh,
        in_specs=(
            P("blk", "dp"),
            P(("blk", "dp"), None),
            P(),
            P(),
            P(("blk", "dp"), None),
            P("dp", None, "blk"),
            P("dp", None, "blk"),
            P("dp", "blk", None),
        ),
        out_specs=P(("blk", "dp"), None),
        check_vma=False,
    )
```

profile of v0, /device:TPU:31, one launch (start us, length us, event | category | flops | bytes accessed | tf_op | source)
XLA Modules:
  0.0 854.9 jit_solution(9166248123100298957)
XLA Ops:
  6.5 0.7 all-gather.4.cloned.1.call-update
  7.3 0.7 all-gather.6.cloned.1.call-update
  8.8 1.5 copy_bitcast_fusion
  10.3 12.0 %all-to-all-start = ((bf16[32,128,224]{1,2,0:T(8,128)(2,1)}), bf16[32,128,224]{1,2,0:T(8,128)(2,1)S(1)}, u32[]{:S(2)}, u32[]{:S(2)}) async-start(bf16[32,128,224]{1,2,0:T(8,128)(2,1)} %copy_bitcast_fusion), calls=%async_computation | async-start | bytes 3670016 | tf_op jit(solution)/shard_map/all_to_all | solution.py:10
  22.8 3.9 copy.63
  27.9 37.8 %all-to-all-done = bf16[32,128,224]{1,2,0:T(8,128)(2,1)S(1)} async-done(((bf16[32,128,224]{1,2,0:T(8,128)(2,1)}), bf16[32,128,224]{1,2,0:T(8,128)(2,1)S(1)}, u32[]{:S(2)}, u32[]{:S(2)}) %all-to-all-start) | async-done | bytes 1835040 | tf_op jit(solution)/shard_map/all_to_all | solution.py:10
  65.7 3.2 multiply_reduce_fusion
  68.9 3.9 multiply_convert_fusion
  72.8 3.9 copy.71
  76.7 5.0 broadcast_in_dim.18
  81.8 8.4 reshape.139
  90.1 10.0 %scatter_custom_fusion = bf16[320,7168]{1,0:T(8,128)(2,1)} fusion(s32[256]{0:T(256)S(1)} %bitcast.97, bf16[256,7168]{1,0:T(8,128)(2,1)} %reshape.139, bf16[]{:T(256)} %constant.38.clone.1), kind=kCustom, calls=%fused_computation.20 | custom fusion | bytes 4588032 | tf_op jit(solution)/shard_map/scatter | solution.py:32
  100.1 7.8 reshape.111
  108.0 169.3 %all_to_all.23 = bf16[32,10,7168]{2,1,0:T(8,128)(2,1)} all-to-all(bf16[32,10,7168]{2,1,0:T(8,128)(2,1)} %reshape.111), channel_id=1, replica_groups=mesh['dp'=32,'blk'=8] {'dp'}, dimensions={0} | all-to-all | bytes 9175040 | tf_op jit(solution)/shard_map/all_to_all | solution.py:33
  277.3 11.3 %fusion.16 = f32[32,1,10,1024]{3,0,2,1:T(8,128)S(1)} fusion(bf16[1,7168,1024]{2,1,0:T(8,128)(2,1)} %all-gather.4.cloned.1.call-done, bf16[32,10,7168]{2,1,0:T(8,128)(2,1)} %all_to_all.23), kind=kOutput, calls=%fused_computation.23 | convolution fusion | flops 4697620480 | bytes 20578304 | tf_op jit(solution)/shard_map/secd,edf->secf/dot_general | solution.py:43
  288.6 133.9 %all-gather.6.cloned.1.call-done = bf16[1,7168,1024]{2,1,0:T(8,128)(2,1)} async-done(((bf16[1,7168,128]{2,1,0:T(8,128)(2,1)}), bf16[1,7168,1024]{2,1,0:T(8,128)(2,1)}) %all-gather.6.cloned.1.call-update) | async-done | bytes 14680080 | tf_op jit(solution)/shard_map/all_gather | solution.py:46
  422.5 14.8 %fusion.36 = bf16[32,10,1024]{2,0,1:T(8,128)(2,1)S(1)} fusion(bf16[1,7168,1024]{2,1,0:T(8,128)(2,1)} %all-gather.6.cloned.1.call-done, bf16[32,10,7168]{2,1,0:T(8,128)(2,1)} %all_to_all.23, f32[32,1,10,1024]{3,0,2,1:T(8,128)S(1)} %fusion.16), kind=kOutput, calls=%fused_computation.27 | convolution fusion | flops 4699586560 | bytes 21233664 | tf_op jit(solution)/shard_map/secd,edf->secf/dot_general | solution.py:43
  437.3 142.1 %all-gather.8.cloned.1.call-done = bf16[1,7168,1024]{2,1,0:T(8,128)(2,1)} async-done(((bf16[1,896,1024]{2,1,0:T(8,128)(2,1)}), bf16[1,7168,1024]{2,1,0:T(8,128)(2,1)}) %all-gather.8.cloned.1.call-update) | async-done | bytes 14680080 | tf_op jit(solution)/shard_map/all_gather | solution.py:51
  579.3 27.1 %fusion.6 = bf16[32,10,7168]{2,0,1:T(8,128)(2,1)} fusion(bf16[32,10,1024]{2,0,1:T(8,128)(2,1)S(1)} %fusion.36, bf16[1,7168,1024]{2,1,0:T(8,128)(2,1)} %all-gather.8.cloned.1.call-done), kind=kOutput, calls=%fused_computation.9 | convolution fusion | flops 4699914240 | bytes 19922944 | tf_op jit(solution)/shard_map/secf,edf->secd/dot_general | solution.py:48
  606.4 8.2 copy.74
  614.6 10.7 %all-to-all-start.2 = ((bf16[32,10,7168]{2,1,0:T(8,128)(2,1)}), bf16[32,10,7168]{2,1,0:T(8,128)(2,1)}, u32[]{:S(2)}, u32[]{:S(2)}) async-start(bf16[32,10,7168]{2,1,0:T(8,128)(2,1)} %copy.74), calls=%async_computation.2 | async-start | bytes 14680064 | tf_op jit(solution)/shard_map/all_to_all | solution.py:55
  625.5 1.9 fusion.43
  627.5 2.0 gather_fusion.1
  629.7 156.1 %all-to-all-done.2 = bf16[32,10,7168]{2,1,0:T(8,128)(2,1)} async-done(((bf16[32,10,7168]{2,1,0:T(8,128)(2,1)}), bf16[32,10,7168]{2,1,0:T(8,128)(2,1)}, u32[]{:S(2)}, u32[]{:S(2)}) %all-to-all-start.2) | async-done | bytes 4587552 | tf_op jit(solution)/shard_map/all_to_all | solution.py:55
  785.8 8.1 reshape.116
  793.9 10.9 %gather_fusion = bf16[256,7168]{1,0:T(8,128)(2,1)} fusion(bf16[320,7168]{1,0:T(8,128)(2,1)} %reshape.116, s32[1024]{0:T(1024)S(1)} %pad_clamp_fusion), kind=kCustom, calls=%fused_computation | custom fusion | bytes 7341056 | tf_op jit(solution)/shard_map/gather | solution.py:58
  804.8 8.1 reshape.117
  812.9 8.9 %fusion.49 = (bf16[128,1,7168]{2,1,0:T(2,128)(2,1)}, bf16[128,1,7168]{2,1,0:T(2,128)(2,1)}) fusion(bf16[128,2,7168]{2,1,0:T(2,128)(2,1)} %reshape.117), kind=kLoop, calls=%fused_computation.52 | loop fusion | bytes 7340032 | tf_op jit(solution)/shard_map/slice | solution.py:61
  821.8 8.4 copy.78
  830.2 8.4 copy.79
  838.6 5.7 fusion.10
  844.3 3.9 copy.77
  (43 shorter events, 2.9 us)
Async XLA Ops:
  6.5 2.2 copy-start
  6.5 270.7 %all-gather.4.cloned.1.call-start = ((), (), s32[]{:S(2)}) async-start(), calls=%async_computation.3 | async-start | bytes 16515072 | tf_op jit(solution)/shard_map/all_gather | solution.py:45
  7.3 415.2 %all-gather.6.cloned.1.call-start = ((), (), s32[]{:S(2)}) async-start(), calls=%async_computation.4 | async-start | bytes 16515072 | tf_op jit(solution)/shard_map/all_gather | solution.py:46
  8.0 571.3 %all-gather.8.cloned.1.call-start = ((), (), s32[]{:S(2)}) async-start(), calls=%async_computation.5 | async-start | bytes 16515072 | tf_op jit(solution)/shard_map/all_gather | solution.py:51
  8.8 13.6 %copy-start.5 = (s32[128,2]{0,1:T(2,128)S(1)}, s32[128,2]{0,1:T(2,128)}, u32[]{:S(2)}) copy-start(s32[128,2]{0,1:T(2,128)} %param.12) | copy-start | bytes 3076
  10.3 16.4 %copy-start.6 = (bf16[7168]{0:T(1024)(128)(2,1)S(1)}, bf16[7168]{0:T(1024)(128)(2,1)}, u32[]{:S(2)}) copy-start(bf16[7168]{0:T(1024)(128)(2,1)} %param.10) | copy-start | bytes 43012
  10.3 55.3 %all-to-all-start = ((bf16[32,128,224]{1,2,0:T(8,128)(2,1)}), bf16[32,128,224]{1,2,0:T(8,128)(2,1)S(1)}, u32[]{:S(2)}, u32[]{:S(2)}) async-start(bf16[32,128,224]{1,2,0:T(8,128)(2,1)} %copy_bitcast_fusion), calls=%async_computation | async-start | bytes 3670016 | tf_op jit(solution)/shard_map/all_to_all | solution.py:10
  65.7 7.1 copy-start.2
  65.7 3.2 copy-start.3
  614.6 11.0 %copy-start.4 = (bf16[7168,32]{0,1:T(8,128)(2,1)S(1)}, bf16[7168,32]{0,1:T(8,128)(2,1)}, u32[]{:S(2)}) copy-start(bf16[7168,32]{0,1:T(8,128)(2,1)} %param.11) | copy-start | bytes 1376260
  614.6 171.3 %all-to-all-start.2 = ((bf16[32,10,7168]{2,1,0:T(8,128)(2,1)}), bf16[32,10,7168]{2,1,0:T(8,128)(2,1)}, u32[]{:S(2)}, u32[]{:S(2)}) async-start(bf16[32,10,7168]{2,1,0:T(8,128)(2,1)} %copy.74), calls=%async_computation.2 | async-start | bytes 14680064 | tf_op jit(solution)/shard_map/all_to_all | solution.py:55
  838.6 9.6 %copy-start.1 = (bf16[4096,224]{0,1:T(8,128)(2,1)S(1)}, bf16[4096,224]{0,1:T(8,128)(2,1)}, u32[]{:S(2)}) copy-start(bf16[4096,224]{0,1:T(8,128)(2,1)} %param.8) | copy-start | bytes 5505028
Sparse Core Ops, SparseCore 0:
  9.1 246.6 all-gather.3
  257.4 164.9 all-gather.5
  424.3 155.0 all-gather.7
where the time goes:
time: 866 us; the launch traced here: 855 us
  waiting for transfers between devices  472 us (55%)
  blocking collectives  169 us (20%)
  local copies, waits for them, and re-layouts  109 us (13%)
  matrix products  55.1 us (6%)
  starting transfers between devices  22.8 us (3%)
  other arithmetic  13.6 us (2%)
  between operations  13.5 us (2%)
    all_to_all x1, blocking collectives, body(): lax.all_to_all(outgoing.reshape(groups, exp_local * capacity, width), 'dp...  169 us
    all_to_all x1, waiting for transfers between devices, body(): lax.all_to_all(results, 'dp', split_axis=0, concat_axis=0, tiled=True)  156 us
    all_gather x1, waiting for transfers between devices, body(): lax.all_gather(down_weight, 'blk', axis=1, tiled=True)  142 us
    all_gather x1, waiting for transfers between devices, body(): upward = project_in(lax.all_gather(up_weight, 'blk', axis=2, tiled=True))  134 us
    all_to_all x1, waiting for transfers between devices, body(): lax.all_to_all(attn_cols, 'dp', split_axis=0, concat_axis=1, tiled=True)  37.8 us
    dot_general x1, matrix products, body(): jnp.einsum('secf,edf->secd', hidden, lax.all_gather(down_weight, 'blk', a...  27.1 us
    dot_general x2, matrix products, project_in(): jnp.einsum('secd,edf->secf', arrived, piece, preferred_element_type=jnp.f...  26.1 us
    unnamed x18, local copies, waits for them, and re-layouts  20.8 us
  transfers between devices with their start and end apart: 5, of which 4 were waited for; matrix products, arithmetic and copies ran while one was open for 9% of the time, Pallas kernels for 0%

commit v1 on v0

v1 whole, which is shorter than its diff:
```python
import jax
import jax.numpy as jnp
from jax import lax
from jax.experimental import pallas as pl
from jax.experimental.pallas import tpu as pltpu
from jax.sharding import PartitionSpec as P

BF = jnp.bfloat16
F32 = jnp.float32
I32 = jnp.int32
D = 7168
FF = 1024
TOK = 128
EXPERTS = 32
CAP = 10
SLOTS = EXPERTS * CAP
PIECE = 224
CHUNK = 896
HALF = D // 2
UNIT = 256
BACK = 144
MESH = pl.DeviceIdType.MESH


def div(a, n):
    return lax.div(a, jnp.int32(n))


def rem(a, n):
    return lax.rem(a, jnp.int32(n))


def shifted(d, k, sign):
    x = rem(div(d, 16) + k // 16, 2)
    z = rem(rem(div(d, 2), 8) + (sign * ((k // 2) % 8) + 8), 8)
    c = rem(rem(d, 2) + k % 2, 2)
    return x * 16 + z * 2 + c


def swap_rows(rows, cols):
    r = lax.broadcasted_iota(I32, (rows, 128), 0)
    outer = lax.shift_right_logical(r * 26215, 21)
    inner = r - outer * 80
    mid = lax.shift_right_logical(inner * 6554, 16)
    last = inner - mid * CAP
    return outer, mid, last, r


def kernel(
    attn,
    residual,
    gain,
    router,
    ids,
    pos,
    pos_t,
    gate,
    up,
    down,
    out,
    gate_all,
    up_all,
    down_all,
    cols,
    stream,
    normed,
    perm,
    perm_back,
    perm_home,
    stack,
    outgoing,
    arrived,
    rows,
    wbuf,
    dbuf,
    acc,
    hidden,
    pile,
    returned,
    coef,
    s_attn,
    r_attn,
    s_ring,
    r_ring,
    s_disp,
    r_disp,
    s_fwd,
    r_fwd,
    s_hid,
    r_hid,
    s_ret,
    r_ret,
    l_sem,
    w_sem,
):
    d = lax.axis_index("dp")
    b = lax.axis_index("blk")
    other = rem(b + 4, 8)
    half = div(b, 4)
    y = rem(b, 4)
    ring_r = half * 4 + rem(y + 1, 4)
    ring_l = half * 4 + rem(y + 3, 4)

    def remote(src, dst, ss, rs, dev):
        return pltpu.make_async_remote_copy(
            src_ref=src,
            dst_ref=dst,
            send_sem=ss,
            recv_sem=rs,
            device_id=dev,
            device_id_type=MESH,
        )

    barrier = pltpu.get_barrier_semaphore()
    for k in range(EXPERTS):
        p = shifted(d, k, 1)
        for q in (b, other):
            if k == 0 and q is b:
                continue
            pl.semaphore_signal(barrier, inc=1, device_id=(p, q), device_id_type=MESH)
    for q in (ring_l, ring_r):
        pl.semaphore_signal(barrier, inc=1, device_id=(d, q), device_id_type=MESH)
    pl.semaphore_wait(barrier, 65)

    attn_out = []
    for k in range(1, 32):
        p = shifted(d, k, 1)
        c = remote(
            attn.at[pl.ds(pl.multiple_of(p * TOK, TOK), TOK)],
            cols.at[d],
            s_attn.at[k],
            r_attn.at[k],
            (p, b),
        )
        c.start()
        attn_out.append(c)
    own_cols = pltpu.make_async_copy(
        attn.at[pl.ds(pl.multiple_of(d * TOK, TOK), TOK)], cols.at[d], l_sem.at[0]
    )
    own_cols.start()
    own_res = pltpu.make_async_copy(residual, normed, l_sem.at[1])
    own_res.start()

    mine = (gate.at[0], up.at[0], down.at[0])
    gathered = (gate_all, up_all, down_all)
    first = []
    for a in range(3):
        c0 = remote(mine[a], gathered[a].at[0], s_ring.at[a, 0], r_ring.at[a, 0], (d, ring_r))
        c1 = remote(mine[a], gathered[a].at[1], s_ring.at[a, 1], r_ring.at[a, 1], (d, ring_l))
        c0.start()
        c1.start()
        first.append((c0, c1))
    second = []

    def pass_on(a):
        n = gathered[a].shape[1] // 2
        c0, c1 = first[a]
        c0.wait_recv()
        f0 = remote(
            gathered[a].at[0, pl.ds(0, n)],
            gathered[a].at[2, pl.ds(0, n)],
            s_ring.at[a, 2],
            r_ring.at[a, 2],
            (d, ring_r),
        )
        f0.start()
        c1.wait_recv()
        f1 = remote(
            gathered[a].at[1, pl.ds(n, n)],
            gathered[a].at[2, pl.ds(n, n)],
            s_ring.at[a, 3],
            r_ring.at[a, 3],
            (d, ring_l),
        )
        f1.start()
        second.append((f0, f1))

    def fetch_in(slot):
        src = mine if slot == 0 else (gate_all.at[slot - 1], up_all.at[slot - 1])
        s = slot % 2
        cs = []
        for i in range(2):
            c = pltpu.make_async_copy(
                src[i], wbuf.at[s, :, pl.ds(i * 128, 128)], w_sem.at[s, i]
            )
            c.start()
            cs.append(c)
        return cs

    def fetch_out(slot):
        src = down.at[0] if slot == 0 else down_all.at[slot - 1]
        s = slot % 2
        c = pltpu.make_async_copy(src, dbuf.at[s], w_sem.at[s, 2])
        c.start()
        return c

    in_copies = {0: fetch_in(0)}
    out_copies = {0: fetch_out(0)}

    outer, mid, last, r = swap_rows(640, 640)
    col = mid * 80 + outer * CAP + last
    lane = lax.broadcasted_iota(I32, (640, 128), 1)
    for j in range(5):
        perm[:, j * 128 : (j + 1) * 128] = jnp.where(lane + j * 128 == col, 1.0, 0.0).astype(BF)
    r = lax.broadcasted_iota(I32, (1152, 128), 0)
    outer = lax.shift_right_logical(r * 14564, 21)
    inner = r - outer * BACK
    mid = lax.shift_right_logical(inner * 6554, 16)
    last = inner - mid * CAP
    col = jnp.where(inner < 140, mid * 80 + outer * CAP + last, -1)
    lane = lax.broadcasted_iota(I32, (1152, 128), 1)
    for j in range(9):
        perm_back[:, j * 128 : (j + 1) * 128] = jnp.where(lane + j * 128 == col, 1.0, 0.0).astype(
            BF
        )
    outer, mid, last, r = swap_rows(1120, 1152)
    col = mid * BACK + outer * CAP + last
    lane = lax.broadcasted_iota(I32, (1120, 128), 1)
    for j in range(9):
        perm_home[:, j * 128 : (j + 1) * 128] = jnp.where(lane + j * 128 == col, 1.0, 0.0).astype(
            BF
        )
    stack_tail = jnp.zeros((32, UNIT), BF)

    for c in attn_out:
        c.wait_recv()
    own_cols.wait()
    own_res.wait()

    def norm_rows(i, carry):
        rs = pl.ds(pl.multiple_of(i * 32, 32), 32)
        total = jnp.zeros((32, 1), F32)
        for q in range(8):
            sl = slice(q * CHUNK, (q + 1) * CHUNK)
            joined = jnp.concatenate([cols[4 * q + m, rs, :] for m in range(4)], axis=1)
            s = normed[rs, sl].astype(F32) + joined.astype(F32)
            stream[rs, sl] = s
            total += jnp.sum(s * s, axis=1, keepdims=True)
        inv = lax.rsqrt(total * (1.0 / D) + 1e-06)
        for q in range(8):
            sl = slice(q * CHUNK, (q + 1) * CHUNK)
            normed[rs, sl] = (stream[rs, sl] * inv * gain[:, sl].astype(F32)).astype(BF)
        return carry

    lax.fori_loop(0, 4, norm_rows, 0)

    def disp_copy(k):
        return remote(
            outgoing.at[pl.ds(pl.multiple_of(k * 80, 80), 80)],
            arrived.at[0, pl.ds(pl.multiple_of(k * 80, 80), 80)],
            s_disp.at[k],
            r_disp.at[k],
            (shifted(d, k, 1), jnp.where(k < 16, b, other)),
        )

    def pick(g):
        want = lax.broadcasted_iota(I32, (80, TOK), 0) + g * 80
        hit = jnp.logical_or(want == pos_t[0:1, :], want == pos_t[1:2, :])
        one = jnp.where(hit, 1.0, 0.0).astype(BF)
        for j in range(8):
            stack[j * 80 : (j + 1) * 80, :] = jnp.dot(
                one, normed[:, j * CHUNK : (j + 1) * CHUNK], preferred_element_type=F32
            ).astype(BF)
        outgoing[pl.ds(pl.multiple_of(g * 640, 640), 640), :] = jnp.dot(
            perm[...], stack[...], preferred_element_type=F32
        ).astype(BF)

    def dispatch(g, carry):
        pick(g)
        for i in range(8):
            k = g * 8 + i

            @pl.when(k > 0)
            def _():
                disp_copy(k).start()

        return carry

    lax.fori_loop(0, 4, dispatch, 0)
    own_rows = pltpu.make_async_copy(
        outgoing.at[pl.ds(0, 80)], arrived.at[0, pl.ds(0, 80)], l_sem.at[2]
    )
    own_rows.start()
    pass_on(0)

    logits = jnp.zeros((TOK, EXPERTS), F32)
    for q in range(8):
        sl = slice(q * CHUNK, (q + 1) * CHUNK)
        logits += jnp.dot(normed[:, sl], router[sl, :], preferred_element_type=F32)
    affinity = jax.nn.sigmoid(logits)
    names = lax.broadcasted_iota(I32, (TOK, EXPERTS), 1)
    chosen = [
        jnp.sum(jnp.where(names == ids[:, m : m + 1], affinity, 0.0), axis=1, keepdims=True)
        for m in range(2)
    ]
    scale = 2.5 / (chosen[0] + chosen[1])
    where = lax.broadcasted_iota(I32, (TOK, SLOTS), 1)
    full = jnp.where(where == pos[:, 0:1], chosen[0] * scale, 0.0) + jnp.where(
        where == pos[:, 1:2], chosen[1] * scale, 0.0
    )
    high = full.astype(BF)
    coef[0:TOK, :] = high
    coef[TOK : 2 * TOK, :] = (full - high.astype(F32)).astype(BF)

    def fwd_copy(k):
        sl = pl.ds(pl.multiple_of(k * 80, 80), 80)
        return remote(arrived.at[0, sl], arrived.at[1, sl], s_fwd.at[k], r_fwd.at[k], (d, other))

    def spread(side, g):
        z = jnp.dot(
            perm[...],
            arrived[side, pl.ds(pl.multiple_of(g * 640, 640), 640), :],
            preferred_element_type=F32,
        ).astype(BF)
        for j in range(8):
            rows[
                pl.ds(pl.multiple_of(side * SLOTS + g * 80, 80), 80),
                j * CHUNK : (j + 1) * CHUNK,
            ] = z[j * 80 : (j + 1) * 80, :]

    own_rows.wait()

    def arrive(g, carry):
        for i in range(8):
            k = g * 8 + i

            @pl.when(k > 0)
            def _():
                disp_copy(k).wait_recv()

            fwd_copy(k).start()
        spread(0, g)
        return carry

    def arrive_other(g, carry):
        for i in range(8):
            fwd_copy(g * 8 + i).wait_recv()
        spread(1, g)
        return carry

    lax.fori_loop(0, 2, arrive, 0)
    pass_on(1)
    in_copies[1] = fetch_in(1)
    lax.fori_loop(2, 3, arrive, 0)
    pass_on(2)
    lax.fori_loop(3, 4, arrive, 0)
    lax.fori_loop(0, 4, arrive_other, 0)

    shard_of = (y, rem(y + 3, 4), rem(y + 1, 4), rem(y + 2, 4))
    for slot in range(4):
        for c in in_copies[slot]:
            c.wait()

        def step(i, carry, slot=slot):
            ks = pl.ds(pl.multiple_of(i * 1024, 1024), 1024)
            part = jnp.dot(rows[:, ks], wbuf[slot % 2, ks, :], preferred_element_type=F32)

            @pl.when(i == 0)
            def _():
                acc[...] = part

            @pl.when(i > 0)
            def _():
                acc[...] += part

            return carry

        lax.fori_loop(0, 7, step, 0)
        g = acc[:, 0:128]
        h = (g / (1.0 + jnp.exp(-g)) * acc[:, 128:256]).astype(BF)
        hidden[0, :, pl.ds(pl.multiple_of(shard_of[slot] * 128, 128), 128)] = h
        if slot + 2 < 4:
            n = slot + 2
            if n == 3:
                for a in range(2):
                    first_r = second[a]
                    first_r[0].wait_recv()
                    first_r[1].wait_recv()
            in_copies[n] = fetch_in(n)
    hid = []
    for i in range(2):
        c = remote(
            hidden.at[0, pl.ds(i * SLOTS, SLOTS)],
            hidden.at[1, pl.ds((1 - i) * SLOTS, SLOTS)],
            s_hid.at[i],
            r_hid.at[1 - i],
            (d, other),
        )
        c.start()
        hid.append(c)
    out_copies[1] = fetch_out(1)
    for c in hid:
        c.wait_recv()

    far = 1 - half
    for slot in range(4):
        out_copies[slot].wait()
        for side in range(2):
            rs = slice(side * SLOTS, (side + 1) * SLOTS)
            res = jnp.zeros((SLOTS, CHUNK), F32)
            for part, at in ((0, half), (1, far)):
                res += lax.dot_general(
                    hidden[part, rs, :],
                    dbuf[slot % 2, :, pl.ds(pl.multiple_of(at * 512, 512), 512)],
                    (((1,), (1,)), ((), ())),
                    preferred_element_type=F32,
                )
            at = pl.multiple_of(shard_of[slot] * CHUNK + side * HALF, 128)
            rows[SLOTS : 2 * SLOTS, pl.ds(at, CHUNK)] = res.astype(BF)
        if slot + 2 < 4:
            if slot + 2 == 3:
                second[2][0].wait_recv()
                second[2][1].wait_recv()
            out_copies[slot + 2] = fetch_out(slot + 2)

    def ret_copy(side, k):
        sl = pl.ds(pl.multiple_of(k * BACK, BACK), BACK)
        near = jnp.where(k < 16, b, other)
        flip = jnp.where(k < 16, other, b)
        return remote(
            wbuf.at[side, sl],
            returned.at[half, sl],
            s_ret.at[side, k],
            r_ret.at[half, k],
            (shifted(d, k, -1), near if side == 0 else flip),
        )

    def ret_wait(h, k):
        sl = pl.ds(pl.multiple_of(k * BACK, BACK), BACK)
        return remote(
            wbuf.at[0, sl],
            returned.at[h, sl],
            s_ret.at[0, k],
            r_ret.at[h, k],
            (shifted(d, k, 1), other),
        )

    stack2 = pile
    stack2[1120:1152, :] = stack_tail

    def send_back(side):
        def body(g, carry):
            for u in range(14):
                at = side * HALF + u * UNIT
                stack2[u * 80 : (u + 1) * 80, :] = rows[
                    pl.ds(pl.multiple_of(SLOTS + g * 80, 80), 80), at : at + UNIT
                ]
            wbuf[side, pl.ds(pl.multiple_of(g * 1152, 1152), 1152), :] = jnp.dot(
                perm_back[...], stack2[...], preferred_element_type=F32
            ).astype(BF)
            for i in range(8):
                k = g * 8 + i
                if side == 0:

                    @pl.when(k > 0)
                    def _():
                        ret_copy(0, k).start()
                else:
                    ret_copy(1, k).start()
            return carry

        lax.fori_loop(0, 4, body, 0)

    send_back(1)
    send_back(0)
    own_back = pltpu.make_async_copy(
        wbuf.at[0, pl.ds(0, BACK)], returned.at[half, pl.ds(0, BACK)], l_sem.at[3]
    )
    own_back.start()
    own_back.wait()

    def home(h):
        def body(g, carry):
            for i in range(8):
                k = g * 8 + i

                @pl.when(jnp.logical_or(k > 0, half != h))
                def _():
                    ret_wait(h, k).wait_recv()

            z = jnp.dot(
                perm_home[...],
                returned[h, pl.ds(pl.multiple_of(g * 1152, 1152), 1152), :],
                preferred_element_type=F32,
            ).astype(BF)
            for u in range(14):
                at = h * HALF + u * UNIT
                rows[pl.ds(pl.multiple_of(g * 80, 80), 80), at : at + UNIT] = z[
                    u * 80 : (u + 1) * 80, :
                ]
            return carry

        lax.fori_loop(0, 4, body, 0)

    home(0)
    home(1)
    for j in range(8):
        sl = slice(j * CHUNK, (j + 1) * CHUNK)
        both = jnp.dot(coef[...], rows[0:SLOTS, sl], preferred_element_type=F32)
        normed[:, sl] = (stream[:, sl] + both[0:TOK, :] + both[TOK : 2 * TOK, :]).astype(BF)
    result = pltpu.make_async_copy(normed, out, l_sem.at[4])
    result.start()

    for c in attn_out:
        c.wait_send()
    for a in range(3):
        first[a][0].wait_send()
        first[a][1].wait_send()
        second[a][0].wait_send()
        second[a][1].wait_send()
    for c in hid:
        c.wait_send()

    def drain(k, carry):
        @pl.when(k > 0)
        def _():
            disp_copy(k).wait_send()
            ret_copy(0, k).wait_send()

        fwd_copy(k).wait_send()
        ret_copy(1, k).wait_send()
        return carry

    lax.fori_loop(0, EXPERTS, drain, 0)
    result.wait()


def layer(attn, residual, gain, router, ids, pos, pos_t, gate, up, down):
    any_ = pl.BlockSpec(memory_space=pl.ANY)
    vmem = pl.BlockSpec(memory_space=pltpu.VMEM)
    dma = pltpu.SemaphoreType.DMA
    got = pl.pallas_call(
        kernel,
        out_shape=[
            jax.ShapeDtypeStruct((TOK, D), BF),
            jax.ShapeDtypeStruct((3, D, 128), BF),
            jax.ShapeDtypeStruct((3, D, 128), BF),
            jax.ShapeDtypeStruct((3, CHUNK, FF), BF),
        ],
        in_specs=[any_, any_, vmem, vmem, vmem, vmem, vmem, any_, any_, any_],
        out_specs=[any_] * 4,
        scratch_shapes=[
            pltpu.VMEM((32, TOK, PIECE), BF),
            pltpu.VMEM((TOK, D), F32),
            pltpu.VMEM((TOK, D), BF),
            pltpu.VMEM((640, 640), BF),
            pltpu.VMEM((1152, 1152), BF),
            pltpu.VMEM((1120, 1152), BF),
            pltpu.VMEM((640, CHUNK), BF),
            pltpu.VMEM((2560, CHUNK), BF),
            pltpu.VMEM((2, 2560, CHUNK), BF),
            pltpu.VMEM((2 * SLOTS, D), BF),
            pltpu.VMEM((2, D, UNIT), BF),
            pltpu.VMEM((2, CHUNK, FF), BF),
            pltpu.VMEM((2 * SLOTS, UNIT), F32),
            pltpu.VMEM((2, 2 * SLOTS, FF // 2), BF),
            pltpu.VMEM((1152, UNIT), BF),
            pltpu.VMEM((2, 32 * BACK, UNIT), BF),
            pltpu.VMEM((2 * TOK, SLOTS), BF),
            dma((32,)),
            dma((32,)),
            dma((3, 4)),
            dma((3, 4)),
            dma((32,)),
            dma((32,)),
            dma((32,)),
            dma((32,)),
            dma((2,)),
            dma((2,)),
            dma((2, 32)),
            dma((2, 32)),
            dma((5,)),
            dma((2, 3)),
        ],
        compiler_params=pltpu.CompilerParams(
            collective_id=0, has_side_effects=True, vmem_limit_bytes=64 * 1024 * 1024 - 4096
        ),
        cost_estimate=pl.CostEstimate(
            flops=20_000_000_000, bytes_accessed=80_000_000, transcendentals=400_000
        ),
    )(attn, residual, gain, router, ids, pos, pos_t, gate, up, down)
    return got[0]


def body(
    attn_cols, residual, norm_gain, router_weight, expert_ids, gate_weight, up_weight, down_weight
):
    d = lax.axis_index("dp")
    flat = expert_ids.reshape(-1)
    n = flat.shape[0]
    earlier = jnp.arange(n)[None, :] < jnp.arange(n)[:, None]
    rank = jnp.sum(
        jnp.logical_and(flat[:, None] == flat[None, :], earlier).astype(I32), axis=1
    ).reshape(expert_ids.shape)
    kx = (expert_ids // 16 - d // 16 + 2) % 2
    kz = ((expert_ids // 2) % 8 - (d // 2) % 8 + 8) % 8
    kc = (expert_ids % 2 - d % 2 + 2) % 2
    pos = (kx * 16 + kz * 2 + kc) * CAP + rank
    return layer(
        attn_cols,
        residual,
        norm_gain.reshape(1, D),
        router_weight,
        expert_ids,
        pos,
        pos.T,
        gate_weight,
        up_weight,
        down_weight,
    )


def solution(mesh):
    return jax.shard_map(
        body,
        mesh=mesh,
        in_specs=(
            P("blk", "dp"),
            P(("blk", "dp"), None),
            P(),
            P(),
            P(("blk", "dp"), None),
            P("dp", None, "blk"),
            P("dp", None, "blk"),
            P("dp", "blk", None),
        ),
        out_specs=P(("blk", "dp"), None),
        check_vma=False,
    )
```

time: 866 us -> 390 us (0.45); the launches traced: 855 us -> 390 us
  waiting for transfers between devices: 472 us -> 0 us
  Pallas kernels: 0 us -> 377 us
  blocking collectives: 169 us -> 0 us
  local copies, waits for them, and re-layouts: 109 us -> 12.3 us
  matrix products: 55.1 us -> 0 us
  starting transfers between devices: 22.8 us -> 0 us
  between operations: 13.5 us -> 0.03 us
  other arithmetic: 13.6 us -> 0.92 us
    pallas_call x0 -> x1, Pallas kernels: none -> 377 us  [layer(): pl.pallas_call(kernel, out_shape=[jax.ShapeDtypeStruct((TOK, D), BF), jax...]
    all_gather x3 -> x0, waiting for transfers between devices: 276 us -> none  [the longest x1 142 us: body(): lax.all_gather(down_weight, 'blk', axis=1, tiled=True)]
    all_to_all x2 -> x0, waiting for transfers between devices: 194 us -> none  [the longest x1 156 us: body(): lax.all_to_all(results, 'dp', split_axis=0, concat_axis=0, tiled=True)]
    all_to_all x1 -> x0, blocking collectives: 169 us -> none  [body(): lax.all_to_all(outgoing.reshape(groups, exp_local * capacity, width), 'dp...]
    dot_general x4 -> x0, matrix products: 55.1 us -> none  [the longest x1 27.1 us: body(): jnp.einsum('secf,edf->secd', hidden, lax.all_gather(down_weight, 'blk', a...]
    reshape x4 -> x3, local copies, waits for them, and re-layouts: 32.5 us -> 1.68 us  [the longest x1 1.47 us: body(): norm_gain.reshape(1, D)]
    all_to_all x2 -> x0, starting transfers between devices: 22.7 us -> none  [the longest x1 12 us: body(): lax.all_to_all(attn_cols, 'dp', split_axis=0, concat_axis=1, tiled=True)]
    convert_element_type x3 -> x0, local copies, waits for them, and re-layouts: 16 us -> none  [the longest x1 8.15 us: body(): produced = jnp.einsum('secf,edf->secd', hidden, lax.all_gather(down_weigh...]
  transfers between devices with their start and end apart: 5 -> 0, of which waited for: 4 -> 0; matrix products, arithmetic and copies ran while one was open for 9% -> 0% of each run, Pallas kernels for 0% -> 0%
where the time goes in v1:
time: 390 us
  Pallas kernels  377 us (97%)
  local copies, waits for them, and re-layouts  12.3 us (3%)
    pallas_call x1, Pallas kernels, layer(): pl.pallas_call(kernel, out_shape=[jax.ShapeDtypeStruct((TOK, D), BF), jax...  377 us
    unnamed x10, local copies, waits for them, and re-layouts  9.76 us

profile of v1, /device:TPU:31, one launch (start us, length us, event | category | flops | bytes accessed | tf_op | source)
XLA Modules:
  0.0 389.8 jit_solution(6241460387719100689)
XLA Ops:
  0.0 0.0 copy-start
  0.0 1.5 reshape.8.gain
  1.5 0.8 copy.23.ids
  2.3 0.0 copy-start.1
  2.3 0.6 copy-done.1
  2.9 0.1 eq.24
  3.0 0.2 convert_reduce_fusion
  3.2 0.1 reshape.9
  3.4 0.1 copy.20
  3.4 0.7 multiply_add_fusion
  4.2 0.0 copy-start.2
  4.2 0.5 copy-done.2
  4.7 0.7 copy.24.pos
  5.4 2.5 copy.22.router
  7.9 0.0 copy-done
  7.9 2.5 copy.21.attn
  10.4 376.6 %shard_map.82 = (bf16[128,7168]{1,0:T(8,128)(2,1)}, bf16[3,7168,128]{2,1,0:T(8,128)(2,1)}, bf16[3,7168,128]{2,1,0:T(8,128)(2,1)}, bf16[3,896,1024]{2,1,0:T(8,128)(2,1)}) custom-call(bf16[4096,224]{1,0:T(8,128)(2,1)} %copy.21.attn, bf16[128,7168]{1,0:T(8,128)(2,1)} %residual.1, bf16[1,7168]{1,0:T(2,128)(2,1)} %reshape.8.gain, bf16[7168,32]{1,0:T(8,128)(2,1)} %copy.22.router, ...), custom_call_target="tpu_custom_call" | custom-call | flops 20000000000 | bytes 80000000 | tf_op jit(solution)/shard_map/pallas_call | solution.py:532
  387.0 2.8 copy.26
Async XLA Ops:
  0.0 7.9 %copy-start = (bf16[4096,224]{0,1:T(8,128)(2,1)S(1)}, bf16[4096,224]{0,1:T(8,128)(2,1)}, u32[]{:S(2)}) copy-start(bf16[4096,224]{0,1:T(8,128)(2,1)} %param.8) | copy-start | bytes 5505028
  2.3 0.6 copy-start.1
  4.2 0.5 copy-start.2

commit v2 on v1

v2 whole, which is shorter than its diff:
```python
import jax
import jax.numpy as jnp
from jax import lax
from jax.experimental import pallas as pl
from jax.experimental.pallas import tpu as pltpu
from jax.sharding import PartitionSpec as P

BF = jnp.bfloat16
F32 = jnp.float32
I32 = jnp.int32
D = 7168
FF = 1024
TOK = 128
EXPERTS = 32
CAP = 10
SLOTS = EXPERTS * CAP
PIECE = 224
CHUNK = 896
HALF = D // 2
UNIT = 256
BACK = 144
MESH = pl.DeviceIdType.MESH


def div(a, n):
    return lax.div(a, jnp.int32(n))


def rem(a, n):
    return lax.rem(a, jnp.int32(n))


def shifted(d, k, sign):
    x = rem(div(d, 16) + k // 16, 2)
    z = rem(rem(div(d, 2), 8) + (sign * ((k // 2) % 8) + 8), 8)
    c = rem(rem(d, 2) + k % 2, 2)
    return x * 16 + z * 2 + c


def nt_dot(a, b):
    return lax.dot_general(a, b, (((1,), (1,)), ((), ())), preferred_element_type=F32)


def rows_at(start, n):
    return pl.ds(pl.multiple_of(start, 16), n)


def kernel(
    attn,
    residual,
    gain,
    router,
    ids,
    gate,
    up,
    down,
    out,
    gate_all,
    up_all,
    down_all,
    cols,
    stream,
    normed,
    gains,
    perm,
    perm_back,
    perm_home,
    stack,
    outgoing,
    arrived,
    rows,
    wbuf,
    dbuf,
    acc,
    hidden,
    pile,
    sending,
    returned,
    coef,
    s_attn,
    r_attn,
    s_ring,
    r_ring,
    s_disp,
    r_disp,
    s_fwd,
    r_fwd,
    s_hid,
    r_hid,
    s_ret,
    r_ret,
    l_sem,
    w_sem,
):
    d = lax.axis_index("dp")
    b = lax.axis_index("blk")
    other = rem(b + 4, 8)
    half = div(b, 4)
    far = 1 - half
    y = rem(b, 4)
    ring_r = half * 4 + rem(y + 1, 4)
    ring_l = half * 4 + rem(y + 3, 4)
    shard_of = (y, rem(y + 3, 4), rem(y + 1, 4), rem(y + 2, 4))

    def remote(src, dst, ss, rs, dev):
        return pltpu.make_async_remote_copy(
            src_ref=src,
            dst_ref=dst,
            send_sem=ss,
            recv_sem=rs,
            device_id=dev,
            device_id_type=MESH,
        )

    def lanes_at(start, n):
        return pl.ds(pl.multiple_of(start, 128), n)

    own_cols = pltpu.make_async_copy(
        attn.at[:, lanes_at(d * TOK, TOK)], cols.at[rows_at(d * PIECE, PIECE)], l_sem.at[0]
    )
    own_cols.start()
    own_res = pltpu.make_async_copy(residual, normed, l_sem.at[1])
    own_res.start()

    barrier = pltpu.get_barrier_semaphore()
    for k in range(EXPERTS):
        p = shifted(d, k, 1)
        for q in (b, other):
            if k == 0 and q is b:
                continue
            pl.semaphore_signal(barrier, inc=1, device_id=(p, q), device_id_type=MESH)
    for q in (ring_l, ring_r):
        pl.semaphore_signal(barrier, inc=1, device_id=(d, q), device_id_type=MESH)
    pl.semaphore_wait(barrier, 65)

    attn_out = []
    for k in range(1, 32):
        p = shifted(d, k, 1)
        c = remote(
            attn.at[:, lanes_at(p * TOK, TOK)],
            cols.at[rows_at(d * PIECE, PIECE)],
            s_attn.at[k],
            r_attn.at[k],
            (p, b),
        )
        c.start()
        attn_out.append(c)

    mine = (gate.at[0], up.at[0], down.at[0])
    gathered = (gate_all, up_all, down_all)
    first = {}
    second = {}

    def begin(a):
        c0 = remote(mine[a], gathered[a].at[0], s_ring.at[a, 0], r_ring.at[a, 0], (d, ring_r))
        c1 = remote(mine[a], gathered[a].at[1], s_ring.at[a, 1], r_ring.at[a, 1], (d, ring_l))
        c0.start()
        c1.start()
        first[a] = (c0, c1)

    def pass_on(a):
        n = gathered[a].shape[1] // 2
        c0, c1 = first[a]
        c0.wait_recv()
        f0 = remote(
            gathered[a].at[0, pl.ds(0, n)],
            gathered[a].at[2, pl.ds(0, n)],
            s_ring.at[a, 2],
            r_ring.at[a, 2],
            (d, ring_r),
        )
        f0.start()
        c1.wait_recv()
        f1 = remote(
            gathered[a].at[1, pl.ds(n, n)],
            gathered[a].at[2, pl.ds(n, n)],
            s_ring.at[a, 3],
            r_ring.at[a, 3],
            (d, ring_l),
        )
        f1.start()
        second[a] = (f0, f1)

    def complete(a):
        second[a][0].wait_recv()
        second[a][1].wait_recv()

    def fetch_in(slot):
        src = mine if slot == 0 else (gate_all.at[slot - 1], up_all.at[slot - 1])
        s = slot % 2
        cs = []
        for i in range(2):
            c = pltpu.make_async_copy(
                src[i], wbuf.at[s, :, pl.ds(i * 128, 128)], w_sem.at[s, i]
            )
            c.start()
            cs.append(c)
        return cs

    def fetch_out(slot):
        src = down.at[0] if slot == 0 else down_all.at[slot - 1]
        s = slot % 2
        c = pltpu.make_async_copy(src, dbuf.at[s], w_sem.at[s, 2])
        c.start()
        return c

    begin(0)
    begin(1)
    in_copies = {0: fetch_in(0)}
    out_copies = {0: fetch_out(0)}

    def fill(i, carry):
        at = rows_at(i * 16, 16)
        r = lax.broadcasted_iota(I32, (16, 128), 0) + i * 16
        lane = lax.broadcasted_iota(I32, (16, 128), 1)
        outer = lax.shift_right_logical(r * 14564, 21)
        inner = r - outer * BACK
        mid = lax.shift_right_logical(inner * 6554, 16)
        back = jnp.where(inner < 140, mid * 80 + outer * CAP + inner - mid * CAP, -1)
        outer = lax.shift_right_logical(r * 26215, 21)
        inner = r - outer * 80
        mid = lax.shift_right_logical(inner * 6554, 16)
        last = inner - mid * CAP
        home = mid * BACK + outer * CAP + last
        swap = mid * 80 + outer * CAP + last
        for j in range(9):
            sl = slice(j * 128, (j + 1) * 128)
            perm_back[at, sl] = jnp.where(lane + j * 128 == back, 1.0, 0.0).astype(BF)
            perm_home[at, sl] = jnp.where(lane + j * 128 == home, 1.0, 0.0).astype(BF)

        @pl.when(i < 40)
        def _():
            for j in range(5):
                sl = slice(j * 128, (j + 1) * 128)
                perm[at, sl] = jnp.where(lane + j * 128 == swap, 1.0, 0.0).astype(BF)

        return carry

    lax.fori_loop(0, 72, fill, 0)
    pile[1120:1152, :] = jnp.zeros((32, UNIT), BF)
    gains[...] = gain[...].astype(F32)

    names = lax.broadcasted_iota(I32, (EXPERTS, TOK), 0)
    named = [names == ids[m : m + 1, :] for m in range(2)]
    uses = jnp.where(jnp.logical_or(named[0], named[1]), 1.0, 0.0).astype(BF)
    t0 = lax.broadcasted_iota(I32, (TOK, TOK), 0)
    t1 = lax.broadcasted_iota(I32, (TOK, TOK), 1)
    eye = jnp.where(t0 == t1, 1.0, 0.0).astype(BF)
    earlier = jnp.dot(uses, jnp.where(t0 < t1, 1.0, 0.0).astype(BF), preferred_element_type=F32)
    ahead = (
        (div(names, 16) - div(d, 16) + 2) % 2 * 16
        + (rem(div(names, 2), 8) - rem(div(d, 2), 8) + 8) % 8 * 2
        + (rem(names, 2) - rem(d, 2) + 2) % 2
    )
    table = ahead.astype(F32) * CAP + earlier
    pos = [
        jnp.sum(jnp.where(named[m], table, 0.0), axis=0, keepdims=True).astype(I32)
        for m in range(2)
    ]

    for c in attn_out:
        c.wait_recv()
    own_cols.wait()
    own_res.wait()
    pass_on(0)

    def add_cols(i, total):
        at = lanes_at(i * UNIT, UNIT)
        s = normed[:, at].astype(F32) + nt_dot(eye, cols[rows_at(i * UNIT, UNIT), :])
        stream[:, at] = s
        sq = s * s
        return total + sq[:, 0:128] + sq[:, 128:256]

    total = lax.fori_loop(0, D // UNIT, add_cols, jnp.zeros((TOK, 128), F32))
    inv = lax.rsqrt(jnp.sum(total, axis=1, keepdims=True) * (1.0 / D) + 1e-06)

    def scale_cols(i, carry):
        at = lanes_at(i * 128, 128)
        normed[:, at] = (stream[:, at] * inv * gains[pl.ds(i, 1), :]).astype(BF)
        return carry

    lax.fori_loop(0, D // 128, scale_cols, 0)

    def disp_copy(k):
        at = rows_at(k * 80, 80)
        return remote(
            outgoing.at[at],
            arrived.at[0, at],
            s_disp.at[k],
            r_disp.at[k],
            (shifted(d, k, 1), jnp.where(k < 16, b, other)),
        )

    def dispatch(g, carry):
        want = lax.broadcasted_iota(I32, (80, TOK), 0) + g * 80
        hit = jnp.logical_or(want == pos[0], want == pos[1])
        one = jnp.where(hit, 1.0, 0.0).astype(BF)
        for j in range(8):
            stack[j * 80 : (j + 1) * 80, :] = jnp.dot(
                one, normed[:, j * CHUNK : (j + 1) * CHUNK], preferred_element_type=F32
            ).astype(BF)
        for n in range(0, CHUNK, UNIT):
            at = slice(n, min(n + UNIT, CHUNK))
            outgoing[rows_at(g * 640, 640), at] = jnp.dot(
                perm[...], stack[:, at], preferred_element_type=F32
            ).astype(BF)
        for i in range(8):
            k = g * 8 + i

            @pl.when(k > 0)
            def _():
                disp_copy(k).start()

        return carry

    lax.fori_loop(0, 4, dispatch, 0)
    own_rows = pltpu.make_async_copy(
        outgoing.at[pl.ds(0, 80)], arrived.at[0, pl.ds(0, 80)], l_sem.at[2]
    )
    own_rows.start()
    begin(2)

    logits = jnp.zeros((EXPERTS, TOK), F32)
    for q in range(8):
        sl = slice(q * CHUNK, (q + 1) * CHUNK)
        logits += nt_dot(router[:, sl], normed[:, sl])
    affinity = jax.nn.sigmoid(logits)
    chosen = [jnp.sum(jnp.where(n, affinity, 0.0), axis=0, keepdims=True) for n in named]
    scale = 2.5 / (chosen[0] + chosen[1])
    for part in range(2):
        where = lax.broadcasted_iota(I32, (160, TOK), 0) + part * 160
        full = jnp.where(where == pos[0], chosen[0] * scale, 0.0) + jnp.where(
            where == pos[1], chosen[1] * scale, 0.0
        )
        high = full.astype(BF)
        low = (full - high.astype(F32)).astype(BF)
        coef[part, 0:TOK, :] = nt_dot(eye, high).astype(BF)
        coef[part, TOK : 2 * TOK, :] = nt_dot(eye, low).astype(BF)

    def fwd_copy(k):
        at = rows_at(k * 80, 80)
        return remote(arrived.at[0, at], arrived.at[1, at], s_fwd.at[k], r_fwd.at[k], (d, other))

    def spread(side, g):
        base = div(g, 2) * SLOTS + side * 160 + rem(g, 2) * 80
        for n in range(0, CHUNK, UNIT):
            m = min(n + UNIT, CHUNK)
            z = jnp.dot(
                perm[...], arrived[side, rows_at(g * 640, 640), n:m], preferred_element_type=F32
            ).astype(BF)
            for j in range(8):
                rows[rows_at(base, 80), j * CHUNK + n : j * CHUNK + m] = z[j * 80 : (j + 1) * 80]

    def arrive(g, carry):
        for i in range(8):
            k = g * 8 + i

            @pl.when(k > 0)
            def _():
                disp_copy(k).wait_recv()

            fwd_copy(k).start()
        spread(0, g)
        return carry

    def arrive_other(g, carry):
        for i in range(8):
            fwd_copy(g * 8 + i).wait_recv()
        spread(1, g)
        return carry

    def project_in(batch):
        at = slice(batch * SLOTS, (batch + 1) * SLOTS)
        for slot in range(4):
            for c in in_copies[slot]:
                c.wait()

            def step(i, carry, slot=slot):
                ks = pl.ds(pl.multiple_of(i * 1024, 1024), 1024)
                part = jnp.dot(rows[at, ks], wbuf[slot % 2, ks, :], preferred_element_type=F32)

                @pl.when(i == 0)
                def _():
                    acc[...] = part

                @pl.when(i > 0)
                def _():
                    acc[...] += part

                return carry

            lax.fori_loop(0, 7, step, 0)
            g = acc[:, 0:128]
            h = (g / (1.0 + jnp.exp(-g)) * acc[:, 128:256]).astype(BF)
            hidden[0, at, lanes_at(shard_of[slot] * 128, 128)] = h
            nxt = slot + 2
            if nxt == 3 and batch == 0:
                complete(0)
                complete(1)
            if nxt < 4:
                in_copies[nxt] = fetch_in(nxt)
            elif batch == 0:
                in_copies[nxt - 4] = fetch_in(nxt - 4)
        cs = []
        for i in range(2):
            c = remote(
                hidden.at[0, pl.ds(batch * SLOTS + i * 160, 160)],
                hidden.at[1, pl.ds(batch * SLOTS + (1 - i) * 160, 160)],
                s_hid.at[batch, i],
                r_hid.at[batch, 1 - i],
                (d, other),
            )
            c.start()
            cs.append(c)
        return cs

    def project_out(batch):
        for slot in range(4):
            out_copies[slot].wait()
            at = slice(batch * SLOTS, (batch + 1) * SLOTS)
            for n in range(0, CHUNK, UNIT):
                w = min(UNIT, CHUNK - n)
                res = nt_dot(
                    hidden[0, at, :], dbuf[slot % 2, n : n + w, lanes_at(half * 512, 512)]
                )
                res += nt_dot(
                    hidden[1, at, :], dbuf[slot % 2, n : n + w, lanes_at(far * 512, 512)]
                )
                for side in range(2):
                    to = lanes_at(shard_of[slot] * CHUNK + side * HALF + n, w)
                    rows[batch * SLOTS : batch * SLOTS + 160, to] = res[
                        side * 160 : (side + 1) * 160
                    ].astype(BF)
            nxt = slot + 2
            if nxt < 4:
                if nxt == 3 and batch == 0:
                    complete(2)
                out_copies[nxt] = fetch_out(nxt)
            elif batch == 0:
                out_copies[nxt - 4] = fetch_out(nxt - 4)

    def ret_copy(side, k):
        at = rows_at(k * BACK, BACK)
        near = jnp.where(k < 16, b, other)
        flip = jnp.where(k < 16, other, b)
        return remote(
            sending.at[side, at],
            returned.at[half, at],
            s_ret.at[side, k],
            r_ret.at[half, k],
            (shifted(d, k, -1), near if side == 0 else flip),
        )

    def ret_wait(h, k):
        at = rows_at(k * BACK, BACK)
        return remote(
            sending.at[0, at],
            returned.at[h, at],
            s_ret.at[0, k],
            r_ret.at[h, k],
            (shifted(d, k, 1), other),
        )

    def send_back(batch):
        for side in (1, 0):

            def body(g, carry, side=side):
                base = batch * SLOTS + (g - batch * 2) * 80
                for u in range(14):
                    at = side * HALF + u * UNIT
                    pile[u * 80 : (u + 1) * 80, :] = rows[rows_at(base, 80), at : at + UNIT]
                sending[side, rows_at(g * 1152, 1152), :] = jnp.dot(
                    perm_back[...], pile[...], preferred_element_type=F32
                ).astype(BF)
                for i in range(8):
                    k = g * 8 + i
                    if side == 0 and batch == 0 and i == 0:

                        @pl.when(k > 0)
                        def _():
                            ret_copy(0, k).start()
                    else:
                        ret_copy(side, k).start()
                return carry

            lax.fori_loop(2 * batch, 2 * batch + 2, body, 0)

    def home(batch):
        for h in range(2):

            def body(g, carry, h=h):
                for i in range(8):
                    k = g * 8 + i
                    if batch == 0 and i == 0:

                        @pl.when(jnp.logical_or(k > 0, half != h))
                        def _():
                            ret_wait(h, k).wait_recv()
                    else:
                        ret_wait(h, k).wait_recv()
                z = jnp.dot(
                    perm_home[0:1120, :],
                    returned[h, rows_at(g * 1152, 1152), :],
                    preferred_element_type=F32,
                ).astype(BF)
                base = batch * SLOTS + 160 + (g - 2 * batch) * 80
                for u in range(14):
                    at = h * HALF + u * UNIT
                    rows[rows_at(base, 80), at : at + UNIT] = z[u * 80 : (u + 1) * 80, :]
                return carry

            lax.fori_loop(2 * batch, 2 * batch + 2, body, 0)

    def combine(batch):
        def body(i, carry):
            at = lanes_at(i * 512, 512)
            both = jnp.dot(
                coef[batch],
                rows[batch * SLOTS + 160 : (batch + 1) * SLOTS, at],
                preferred_element_type=F32,
            )
            s = stream[:, at] + both[0:TOK, :] + both[TOK : 2 * TOK, :]
            if batch == 0:
                stream[:, at] = s
            else:
                normed[:, at] = s.astype(BF)
            return carry

        lax.fori_loop(0, D // 512, body, 0)

    own_rows.wait()
    lax.fori_loop(0, 1, arrive, 0)
    pass_on(1)
    in_copies[1] = fetch_in(1)
    lax.fori_loop(1, 2, arrive, 0)
    lax.fori_loop(0, 2, arrive_other, 0)
    pass_on(2)
    out_copies[1] = fetch_out(1)
    hid_a = project_in(0)
    lax.fori_loop(2, 3, arrive, 0)
    for c in hid_a:
        c.wait_recv()
    project_out(0)
    send_back(0)
    own_back = pltpu.make_async_copy(
        sending.at[0, pl.ds(0, BACK)], returned.at[half, pl.ds(0, BACK)], l_sem.at[3]
    )
    own_back.start()
    lax.fori_loop(3, 4, arrive, 0)
    lax.fori_loop(2, 4, arrive_other, 0)
    hid_b = project_in(1)
    for c in hid_b:
        c.wait_recv()
    project_out(1)
    send_back(1)
    own_back.wait()
    home(0)
    combine(0)
    home(1)
    combine(1)
    result = pltpu.make_async_copy(normed, out, l_sem.at[4])
    result.start()

    for c in attn_out:
        c.wait_send()
    for a in range(3):
        for c in first[a] + second[a]:
            c.wait_send()
    for c in hid_a + hid_b:
        c.wait_send()

    def drain(k, carry):
        @pl.when(k > 0)
        def _():
            disp_copy(k).wait_send()
            ret_copy(0, k).wait_send()

        fwd_copy(k).wait_send()
        ret_copy(1, k).wait_send()
        return carry

    lax.fori_loop(0, EXPERTS, drain, 0)
    result.wait()


def layer(attn, residual, gain, router, ids, gate, up, down):
    any_ = pl.BlockSpec(memory_space=pl.ANY)
    vmem = pl.BlockSpec(memory_space=pltpu.VMEM)
    dma = pltpu.SemaphoreType.DMA
    got = pl.pallas_call(
        kernel,
        out_shape=[
            jax.ShapeDtypeStruct((TOK, D), BF),
            jax.ShapeDtypeStruct((3, D, 128), BF),
            jax.ShapeDtypeStruct((3, D, 128), BF),
            jax.ShapeDtypeStruct((3, CHUNK, FF), BF),
        ],
        in_specs=[any_, any_, vmem, vmem, vmem, any_, any_, any_],
        out_specs=[any_] * 4,
        scratch_shapes=[
            pltpu.VMEM((D, TOK), BF),
            pltpu.VMEM((TOK, D), F32),
            pltpu.VMEM((TOK, D), BF),
            pltpu.VMEM((56, 128), F32),
            pltpu.VMEM((640, 640), BF),
            pltpu.VMEM((1152, 1152), BF),
            pltpu.VMEM((1152, 1152), BF),
            pltpu.VMEM((640, CHUNK), BF),
            pltpu.VMEM((2560, CHUNK), BF),
            pltpu.VMEM((2, 2560, CHUNK), BF),
            pltpu.VMEM((2 * SLOTS, D), BF),
            pltpu.VMEM((2, D, UNIT), BF),
            pltpu.VMEM((2, CHUNK, FF), BF),
            pltpu.VMEM((SLOTS, UNIT), F32),
            pltpu.VMEM((2, 2 * SLOTS, FF // 2), BF),
            pltpu.VMEM((1152, UNIT), BF),
            pltpu.VMEM((2, 32 * BACK, UNIT), BF),
            pltpu.VMEM((2, 32 * BACK, UNIT), BF),
            pltpu.VMEM((2, 2 * TOK, 160), BF),
            dma((32,)),
            dma((32,)),
            dma((3, 4)),
            dma((3, 4)),
            dma((32,)),
            dma((32,)),
            dma((32,)),
            dma((32,)),
            dma((2, 2)),
            dma((2, 2)),
            dma((2, 32)),
            dma((2, 32)),
            dma((5,)),
            dma((2, 3)),
        ],
        compiler_params=pltpu.CompilerParams(
            collective_id=0, has_side_effects=True, vmem_limit_bytes=64 * 1024 * 1024 - 4096
        ),
        cost_estimate=pl.CostEstimate(
            flops=20_000_000_000, bytes_accessed=80_000_000, transcendentals=400_000
        ),
    )(attn, residual, gain, router, ids, gate, up, down)
    return got[0]


def body(
    attn_cols, residual, norm_gain, router_weight, expert_ids, gate_weight, up_weight, down_weight
):
    return layer(
        attn_cols.T,
        residual,
        norm_gain.reshape(D // 128, 128),
        router_weight.T,
        expert_ids.T,
        gate_weight,
        up_weight,
        down_weight,
    )


def solution(mesh):
    return jax.shard_map(
        body,
        mesh=mesh,
        in_specs=(
            P("blk", "dp"),
            P(("blk", "dp"), None),
            P(),
            P(),
            P(("blk", "dp"), None),
            P("dp", None, "blk"),
            P("dp", None, "blk"),
            P("dp", "blk", None),
        ),
        out_specs=P(("blk", "dp"), None),
        check_vma=False,
    )
```

time: 390 us -> 350 us (0.90)
  Pallas kernels: 377 us -> 344 us
  local copies, waits for them, and re-layouts: 12.3 us -> 2.85 us
    pallas_call x1, Pallas kernels: 377 us -> 344 us  [layer(): pl.pallas_call(kernel, out_shape=[jax.ShapeDtypeStruct((TOK, D), BF), jax...]
    unnamed x10 -> x1, local copies, waits for them, and re-layouts: 9.76 us -> 2.85 us
where the time goes in v2:
time: 350 us; the launch traced here: 347 us
  Pallas kernels  344 us (98%)
    pallas_call x1, Pallas kernels, layer(): pl.pallas_call(kernel, out_shape=[jax.ShapeDtypeStruct((TOK, D), BF), jax...  344 us

profile of v2, /device:TPU:31, one launch (start us, length us, event | category | flops | bytes accessed | tf_op | source)
XLA Modules:
  0.0 346.9 jit_solution(15229618781293925468)
XLA Ops:
  0.0 344.0 %shard_map.82 = (bf16[128,7168]{1,0:T(8,128)(2,1)}, bf16[3,7168,128]{2,1,0:T(8,128)(2,1)}, bf16[3,7168,128]{2,1,0:T(8,128)(2,1)}, bf16[3,896,1024]{2,1,0:T(8,128)(2,1)}) custom-call(bf16[224,4096]{1,0:T(8,128)(2,1)} %bitcast.4, bf16[128,7168]{1,0:T(8,128)(2,1)} %residual.1, bf16[56,128]{1,0:T(8,128)(2,1)} %bitcast.6, bf16[32,7168]{1,0:T(8,128)(2,1)} %bitcast.5, ...), custom_call_target="tpu_custom_call" | custom-call | flops 20000000000 | bytes 80000000 | tf_op jit(solution)/shard_map/pallas_call | solution.py:590
  344.0 2.8 copy.10

commit v3 on v2

--- a/solution.py
+++ b/solution.py
@@ -32,7 +32,9 @@
 
 def shifted(d, k, sign):
     x = rem(div(d, 16) + k // 16, 2)
-    z = rem(rem(div(d, 2), 8) + (sign * ((k // 2) % 8) + 8), 8)
+    i = (k // 2) % 8
+    step = (i % 2) * ((i + 1) // 2) + (1 - i % 2) * ((8 - i // 2) % 8)
+    z = rem(rem(div(d, 2), 8) + (sign * step + 8), 8)
     c = rem(rem(d, 2) + k % 2, 2)
     return x * 16 + z * 2 + c
 
@@ -204,8 +206,8 @@
         c.start()
         return c
 
-    begin(0)
-    begin(1)
+    for a in range(3):
+        begin(a)
     in_copies = {0: fetch_in(0)}
     out_copies = {0: fetch_out(0)}
 
@@ -247,9 +249,11 @@
     t1 = lax.broadcasted_iota(I32, (TOK, TOK), 1)
     eye = jnp.where(t0 == t1, 1.0, 0.0).astype(BF)
     earlier = jnp.dot(uses, jnp.where(t0 < t1, 1.0, 0.0).astype(BF), preferred_element_type=F32)
+    step = (rem(div(names, 2), 8) - rem(div(d, 2), 8) + 8) % 8
+    order = jnp.where(step > 4, 16 - 2 * step, jnp.maximum(2 * step - 1, 0))
     ahead = (
         (div(names, 16) - div(d, 16) + 2) % 2 * 16
-        + (rem(div(names, 2), 8) - rem(div(d, 2), 8) + 8) % 8 * 2
+        + order * 2
         + (rem(names, 2) - rem(d, 2) + 2) % 2
     )
     table = ahead.astype(F32) * CAP + earlier
@@ -288,7 +292,7 @@
             arrived.at[0, at],
             s_disp.at[k],
             r_disp.at[k],
-            (shifted(d, k, 1), jnp.where(k < 16, b, other)),
+            (shifted(d, k, 1), jnp.where(jnp.int32(k) < 16, b, other)),
         )
 
     def dispatch(g, carry):
@@ -318,7 +322,6 @@
         outgoing.at[pl.ds(0, 80)], arrived.at[0, pl.ds(0, 80)], l_sem.at[2]
     )
     own_rows.start()
-    begin(2)
 
     logits = jnp.zeros((EXPERTS, TOK), F32)
     for q in range(8):
@@ -342,7 +345,7 @@
         return remote(arrived.at[0, at], arrived.at[1, at], s_fwd.at[k], r_fwd.at[k], (d, other))
 
     def spread(side, g):
-        base = div(g, 2) * SLOTS + side * 160 + rem(g, 2) * 80
+        base = (g // 2) * SLOTS + side * 160 + (g % 2) * 80
         for n in range(0, CHUNK, UNIT):
             m = min(n + UNIT, CHUNK)
             z = jnp.dot(
@@ -351,17 +354,11 @@
             for j in range(8):
                 rows[rows_at(base, 80), j * CHUNK + n : j * CHUNK + m] = z[j * 80 : (j + 1) * 80]
 
-    def arrive(g, carry):
-        for i in range(8):
-            k = g * 8 + i
-
-            @pl.when(k > 0)
-            def _():
+    def take(first_k, n):
+        for k in range(first_k, first_k + n):
+            if k > 0:
                 disp_copy(k).wait_recv()
-
             fwd_copy(k).start()
-        spread(0, g)
-        return carry
 
     def arrive_other(g, carry):
         for i in range(8):
@@ -369,38 +366,31 @@
         spread(1, g)
         return carry
 
-    def project_in(batch):
+    def project_in(batch, slot):
         at = slice(batch * SLOTS, (batch + 1) * SLOTS)
-        for slot in range(4):
-            for c in in_copies[slot]:
-                c.wait()
-
-            def step(i, carry, slot=slot):
-                ks = pl.ds(pl.multiple_of(i * 1024, 1024), 1024)
-                part = jnp.dot(rows[at, ks], wbuf[slot % 2, ks, :], preferred_element_type=F32)
-
-                @pl.when(i == 0)
-                def _():
-                    acc[...] = part
-
-                @pl.when(i > 0)
-                def _():
-                    acc[...] += part
-
-                return carry
-
-            lax.fori_loop(0, 7, step, 0)
-            g = acc[:, 0:128]
-            h = (g / (1.0 + jnp.exp(-g)) * acc[:, 128:256]).astype(BF)
-            hidden[0, at, lanes_at(shard_of[slot] * 128, 128)] = h
-            nxt = slot + 2
-            if nxt == 3 and batch == 0:
-                complete(0)
-                complete(1)
-            if nxt < 4:
-                in_copies[nxt] = fetch_in(nxt)
-            elif batch == 0:
-                in_copies[nxt - 4] = fetch_in(nxt - 4)
+        for c in in_copies[slot]:
+            c.wait()
+
+        def step(i, carry):
+            ks = pl.ds(pl.multiple_of(i * 1024, 1024), 1024)
+            part = jnp.dot(rows[at, ks], wbuf[slot % 2, ks, :], preferred_element_type=F32)
+
+            @pl.when(i == 0)
+            def _():
+                acc[...] = part
+
+            @pl.when(i > 0)
+            def _():
+                acc[...] += part
+
+            return carry
+
+        lax.fori_loop(0, 7, step, 0)
+        g = acc[:, 0:128]
+        h = (g / (1.0 + jnp.exp(-g)) * acc[:, 128:256]).astype(BF)
+        hidden[0, at, lanes_at(shard_of[slot] * 128, 128)] = h
+
+    def swap_hidden(batch):
         cs = []
         for i in range(2):
             c = remote(
@@ -431,13 +421,16 @@
                     rows[batch * SLOTS : batch * SLOTS + 160, to] = res[
                         side * 160 : (side + 1) * 160
                     ].astype(BF)
-            nxt = slot + 2
-            if nxt < 4:
-                if nxt == 3 and batch == 0:
-                    complete(2)
-                out_copies[nxt] = fetch_out(nxt)
-            elif batch == 0:
-                out_copies[nxt - 4] = fetch_out(nxt - 4)
+            if slot == 0:
+                out_copies[2] = fetch_out(2)
+            elif slot == 2 and batch == 0:
+                complete(2)
+                out_copies[3] = fetch_out(3)
+                out_copies[0] = fetch_out(0)
+            elif slot == 1 and batch == 1:
+                out_copies[3] = fetch_out(3)
+            elif slot == 3 and batch == 0:
+                out_copies[1] = fetch_out(1)
 
     def ret_copy(side, k):
         at = rows_at(k * BACK, BACK)
@@ -529,15 +522,30 @@
         lax.fori_loop(0, D // 512, body, 0)
 
     own_rows.wait()
-    lax.fori_loop(0, 1, arrive, 0)
+    take(0, 8)
     pass_on(1)
     in_copies[1] = fetch_in(1)
-    lax.fori_loop(1, 2, arrive, 0)
+    spread(0, 0)
+    take(8, 8)
+    spread(0, 1)
     lax.fori_loop(0, 2, arrive_other, 0)
     pass_on(2)
     out_copies[1] = fetch_out(1)
-    hid_a = project_in(0)
-    lax.fori_loop(2, 3, arrive, 0)
+    take(16, 4)
+    project_in(0, 0)
+    in_copies[2] = fetch_in(2)
+    project_in(0, 1)
+    project_in(0, 2)
+    in_copies[0] = fetch_in(0)
+    take(20, 4)
+    complete(0)
+    complete(1)
+    in_copies[3] = fetch_in(3)
+    spread(0, 2)
+    project_in(0, 3)
+    in_copies[1] = fetch_in(1)
+    hid_a = swap_hidden(0)
+    take(24, 4)
     for c in hid_a:
         c.wait_recv()
     project_out(0)
@@ -546,9 +554,16 @@
         sending.at[0, pl.ds(0, BACK)], returned.at[half, pl.ds(0, BACK)], l_sem.at[3]
     )
     own_back.start()
-    lax.fori_loop(3, 4, arrive, 0)
+    take(28, 4)
+    spread(0, 3)
     lax.fori_loop(2, 4, arrive_other, 0)
-    hid_b = project_in(1)
+    project_in(1, 0)
+    in_copies[2] = fetch_in(2)
+    project_in(1, 1)
+    in_copies[3] = fetch_in(3)
+    project_in(1, 2)
+    project_in(1, 3)
+    hid_b = swap_hidden(1)
     for c in hid_b:
         c.wait_recv()
     project_out(1)

time: 350 us -> 336 us (0.960)
  Pallas kernels: 344 us -> 327 us
    pallas_call x1, Pallas kernels: 344 us -> 327 us  [layer(): pl.pallas_call(kernel, out_shape=[jax.ShapeDtypeStruct((TOK, D), BF), jax...]
where the time goes in v3:
time: 336 us; the launch traced here: 330 us
  Pallas kernels  327 us (97%)
    pallas_call x1, Pallas kernels, layer(): pl.pallas_call(kernel, out_shape=[jax.ShapeDtypeStruct((TOK, D), BF), jax...  327 us

profile of v3, /device:TPU:31, one launch (start us, length us, event | category | flops | bytes accessed | tf_op | source)
XLA Modules:
  0.0 329.6 jit_solution(11939767669460072977)
XLA Ops:
  0.0 326.8 %shard_map.82 = (bf16[128,7168]{1,0:T(8,128)(2,1)}, bf16[3,7168,128]{2,1,0:T(8,128)(2,1)}, bf16[3,7168,128]{2,1,0:T(8,128)(2,1)}, bf16[3,896,1024]{2,1,0:T(8,128)(2,1)}) custom-call(bf16[224,4096]{1,0:T(8,128)(2,1)} %bitcast.4, bf16[128,7168]{1,0:T(8,128)(2,1)} %residual.1, bf16[56,128]{1,0:T(8,128)(2,1)} %bitcast.6, bf16[32,7168]{1,0:T(8,128)(2,1)} %bitcast.5, ...), custom_call_target="tpu_custom_call" | custom-call | flops 20000000000 | bytes 80000000 | tf_op jit(solution)/shard_map/pallas_call | solution.py:605
  326.8 2.8 copy.10

commit v4 on v3

--- a/solution.py
+++ b/solution.py
@@ -19,6 +19,7 @@
 HALF = D // 2
 UNIT = 256
 BACK = 144
+AHEAD = 7
 MESH = pl.DeviceIdType.MESH
 
 
@@ -262,11 +263,10 @@
         for m in range(2)
     ]
 
-    for c in attn_out:
+    for c in attn_out[:15]:
         c.wait_recv()
     own_cols.wait()
     own_res.wait()
-    pass_on(0)
 
     def add_cols(i, total):
         at = lanes_at(i * UNIT, UNIT)
@@ -275,7 +275,12 @@
         sq = s * s
         return total + sq[:, 0:128] + sq[:, 128:256]
 
-    total = lax.fori_loop(0, D // UNIT, add_cols, jnp.zeros((TOK, 128), F32))
+    near = div(d, 16) * 14
+    total = lax.fori_loop(near, near + 14, add_cols, jnp.zeros((TOK, 128), F32))
+    for c in attn_out[15:]:
+        c.wait_recv()
+    pass_on(0)
+    total = lax.fori_loop(14 - near, 28 - near, add_cols, total)
     inv = lax.rsqrt(jnp.sum(total, axis=1, keepdims=True) * (1.0 / D) + 1e-06)
 
     def scale_cols(i, carry):
@@ -311,7 +316,7 @@
         for i in range(8):
             k = g * 8 + i
 
-            @pl.when(k > 0)
+            @pl.when(jnp.logical_and(k > 0, k <= AHEAD))
             def _():
                 disp_copy(k).start()
 
@@ -359,6 +364,9 @@
             if k > 0:
                 disp_copy(k).wait_recv()
             fwd_copy(k).start()
+            if k > 0 and k + AHEAD < EXPERTS:
+                disp_copy(k).wait_send()
+                disp_copy(k + AHEAD).start()
 
     def arrive_other(g, carry):
         for i in range(8):
@@ -528,10 +536,12 @@
     spread(0, 0)
     take(8, 8)
     spread(0, 1)
-    lax.fori_loop(0, 2, arrive_other, 0)
+    take(16, 2)
+    arrive_other(0, 0)
+    take(18, 2)
+    arrive_other(1, 0)
     pass_on(2)
     out_copies[1] = fetch_out(1)
-    take(16, 4)
     project_in(0, 0)
     in_copies[2] = fetch_in(2)
     project_in(0, 1)
@@ -545,7 +555,8 @@
     project_in(0, 3)
     in_copies[1] = fetch_in(1)
     hid_a = swap_hidden(0)
-    take(24, 4)
+    take(24, 8)
+    spread(0, 3)
     for c in hid_a:
         c.wait_recv()
     project_out(0)
@@ -554,8 +565,6 @@
         sending.at[0, pl.ds(0, BACK)], returned.at[half, pl.ds(0, BACK)], l_sem.at[3]
     )
     own_back.start()
-    take(28, 4)
-    spread(0, 3)
     lax.fori_loop(2, 4, arrive_other, 0)
     project_in(1, 0)
     in_copies[2] = fetch_in(2)
@@ -587,8 +596,11 @@
     def drain(k, carry):
         @pl.when(k > 0)
         def _():
+            ret_copy(0, k).wait_send()
+
+        @pl.when(k >= EXPERTS - AHEAD)
+        def _():
             disp_copy(k).wait_send()
-            ret_copy(0, k).wait_send()
 
         fwd_copy(k).wait_send()
         ret_copy(1, k).wait_send()

time: 336 us -> 322 us (0.958); the launches traced: 330 us -> 319 us
  Pallas kernels: 327 us -> 316 us
    pallas_call x1, Pallas kernels: 327 us -> 316 us  [layer(): pl.pallas_call(kernel, out_shape=[jax.ShapeDtypeStruct((TOK, D), BF), jax...]
where the time goes in v4:
time: 322 us; the launch traced here: 319 us
  Pallas kernels  316 us (98%)
    pallas_call x1, Pallas kernels, layer(): pl.pallas_call(kernel, out_shape=[jax.ShapeDtypeStruct((TOK, D), BF), jax...  316 us

profile of v4, /device:TPU:31, one launch (start us, length us, event | category | flops | bytes accessed | tf_op | source)
XLA Modules:
  0.0 319.2 jit_solution(11989067525037783208)
XLA Ops:
  0.0 316.4 %shard_map.82 = (bf16[128,7168]{1,0:T(8,128)(2,1)}, bf16[3,7168,128]{2,1,0:T(8,128)(2,1)}, bf16[3,7168,128]{2,1,0:T(8,128)(2,1)}, bf16[3,896,1024]{2,1,0:T(8,128)(2,1)}) custom-call(bf16[224,4096]{1,0:T(8,128)(2,1)} %bitcast.4, bf16[128,7168]{1,0:T(8,128)(2,1)} %residual.1, bf16[56,128]{1,0:T(8,128)(2,1)} %bitcast.6, bf16[32,7168]{1,0:T(8,128)(2,1)} %bitcast.5, ...), custom_call_target="tpu_custom_call" | custom-call | flops 20000000000 | bytes 80000000 | tf_op jit(solution)/shard_map/pallas_call | solution.py:617
  316.4 2.8 copy.10

commit v5 on v4

--- a/solution.py
+++ b/solution.py
@@ -412,8 +412,8 @@
             cs.append(c)
         return cs
 
-    def project_out(batch):
-        for slot in range(4):
+    def project_out(batch, slots):
+        for slot in slots:
             out_copies[slot].wait()
             at = slice(batch * SLOTS, (batch + 1) * SLOTS)
             for n in range(0, CHUNK, UNIT):
@@ -432,8 +432,6 @@
             if slot == 0:
                 out_copies[2] = fetch_out(2)
             elif slot == 2 and batch == 0:
-                complete(2)
-                out_copies[3] = fetch_out(3)
                 out_copies[0] = fetch_out(0)
             elif slot == 1 and batch == 1:
                 out_copies[3] = fetch_out(3)
@@ -555,16 +553,20 @@
     project_in(0, 3)
     in_copies[1] = fetch_in(1)
     hid_a = swap_hidden(0)
-    take(24, 8)
-    spread(0, 3)
+    take(24, 4)
     for c in hid_a:
         c.wait_recv()
-    project_out(0)
+    project_out(0, (0, 1, 2))
+    take(28, 4)
+    complete(2)
+    out_copies[3] = fetch_out(3)
+    project_out(0, (3,))
     send_back(0)
     own_back = pltpu.make_async_copy(
         sending.at[0, pl.ds(0, BACK)], returned.at[half, pl.ds(0, BACK)], l_sem.at[3]
     )
     own_back.start()
+    spread(0, 3)
     lax.fori_loop(2, 4, arrive_other, 0)
     project_in(1, 0)
     in_copies[2] = fetch_in(2)
@@ -575,7 +577,7 @@
     hid_b = swap_hidden(1)
     for c in hid_b:
         c.wait_recv()
-    project_out(1)
+    project_out(1, range(4))
     send_back(1)
     own_back.wait()
     home(0)

time: 322 us -> 324 us (level)
  no operation moved by 1% of the time
where the time goes in v5:
time: 324 us; the launch traced here: 320 us
  Pallas kernels  317 us (98%)
    pallas_call x1, Pallas kernels, layer(): pl.pallas_call(kernel, out_shape=[jax.ShapeDtypeStruct((TOK, D), BF), jax...  317 us

profile of v5, /device:TPU:31, one launch (start us, length us, event | category | flops | bytes accessed | tf_op | source)
XLA Modules:
  0.0 320.2 jit_solution(15330013599176266290)
XLA Ops:
  0.0 317.4 %shard_map.82 = (bf16[128,7168]{1,0:T(8,128)(2,1)}, bf16[3,7168,128]{2,1,0:T(8,128)(2,1)}, bf16[3,7168,128]{2,1,0:T(8,128)(2,1)}, bf16[3,896,1024]{2,1,0:T(8,128)(2,1)}) custom-call(bf16[224,4096]{1,0:T(8,128)(2,1)} %bitcast.4, bf16[128,7168]{1,0:T(8,128)(2,1)} %residual.1, bf16[56,128]{1,0:T(8,128)(2,1)} %bitcast.6, bf16[32,7168]{1,0:T(8,128)(2,1)} %bitcast.5, ...), custom_call_target="tpu_custom_call" | custom-call | flops 20000000000 | bytes 80000000 | tf_op jit(solution)/shard_map/pallas_call | solution.py:619
  317.4 2.8 copy.10
